TPU v7x, 512 devices: a whole 4x8x8 slice. The times are simulated.
512 devices in a mesh: rows: 32 (over x, y), tp: 16 (over z, core).
Axes of the slice: x: 4, y: 8, z: 8, core: 2. Of those that a mesh axis runs over, the one named last changes fastest.
Arguments:
- queries: bfloat16 [8192, 8192], P('rows', 'tp'), may hold values from -32 to 32
- nbr_keys: bfloat16 [32768, 8192], P(('rows', 'tp')), may hold values from -8 to 8
- nbr_values: bfloat16 [32768, 8192], P(('rows', 'tp')), may hold values from -15 to 15
- nbr_index: int32 [128, 2], P('rows'), may hold values from 0 to 7, all different within a row
- residual: bfloat16 [8192, 8192], P(('rows', 'tp')), may hold values from -2 to 2
- out_weight: bfloat16 [8192, 8192], P('tp', 'rows'), may hold values from -0.0625 to 0.0625
Outputs:
- mixed: bfloat16 [8192, 8192], P(('rows', 'tp'))
Inputs may be any that keep to these rules, and one draw needn't show every extreme that they name: `nbr_index`: the 2 entries of a span differ; they index the 8 neighbours retrieved for that span's own sequence shard.
All inputs are finite; a program needn't handle non-finite values.
Results may differ from a plain program's by a relative error of at most 0.022.
Values may be sent and summed in bfloat16 or wider, within the bound.
A program may use at most 64 MiB of HBM per device.

v0:
```python
import math
import jax
import jax.numpy as jnp
from jax import lax
from jax.sharding import PartitionSpec as P

HD = 128
CH = 64
R = 128


def shards(queries, nbr_keys, nbr_values, nbr_index, residual, out_weight):
    keys_local, values_local = (
        lax.all_to_all(nbr_keys, "tp", split_axis=1, concat_axis=0, tiled=True),
        lax.all_to_all(nbr_values, "tp", split_axis=1, concat_axis=0, tiled=True),
    )
    heads_local = queries.shape[1] // HD
    span_count = queries.shape[0] // CH
    neighbour_count = keys_local.shape[0] // R
    score_scale = 1.0 / math.sqrt(HD)
    query_blocks = queries.reshape(span_count, CH, heads_local, HD)
    key_blocks = keys_local.reshape(neighbour_count, R, heads_local, HD)[nbr_index]
    value_blocks = values_local.reshape(neighbour_count, R, heads_local, HD)[nbr_index]
    scores = (
        jnp.einsum(
            "cqhd,ckrhd->chqkr", query_blocks, key_blocks, preferred_element_type=jnp.float32
        )
        * score_scale
    )
    row_top = jnp.max(scores, axis=(3, 4), keepdims=True)
    weights = jnp.exp(scores - row_top)
    probs = (weights / jnp.sum(weights, axis=(3, 4), keepdims=True)).astype(jnp.bfloat16)
    attended = jnp.einsum(
        "chqkr,ckrhd->cqhd", probs, value_blocks, preferred_element_type=jnp.float32
    )
    attn = attended.astype(jnp.bfloat16).reshape(queries.shape[0], heads_local * HD)
    partial_value = jnp.dot(
        attn,
        lax.all_gather(out_weight, "rows", axis=1, tiled=True),
        preferred_element_type=jnp.float32,
    )
    summed = lax.psum_scatter(
        partial_value.astype(jnp.bfloat16), "tp", scatter_dimension=0, tiled=True
    ).astype(jnp.float32)
    return (residual.astype(jnp.float32) + summed).astype(jnp.bfloat16)


def solution(mesh):
    placed = (
        P("rows", "tp"),
        P(("rows", "tp"), None),
        P(("rows", "tp"), None),
        P("rows", None),
        P(("rows", "tp"), None),
        P("tp", "rows"),
    )
    return jax.shard_map(
        shards, mesh=mesh, in_specs=placed, out_specs=P(("rows", "tp"), None), check_vma=False
    )
```

profile of v0, /device:TPU:8, one launch (start us, length us, event | category | flops | bytes accessed | tf_op | source)
XLA Modules:
  0.0 204.7 jit_solution(4204165510992683133)
XLA Ops:
  6.5 0.0 copy-start.3
  6.5 0.0 copy-start.2
  6.5 0.0 all-gather.2.cloned.1.call-start
  6.5 0.7 all-gather.2.cloned.1.call-update
  7.3 2.3 %copy.46 = bf16[8,16,8,512]{3,2,0,1:T(8,128)(2,1)} copy(bf16[8,16,8,512]{3,2,1,0:T(8,128)(2,1)} %bitcast.35) | data formatting | bytes 2097152 | tf_op jit(solution)/shard_map/all_to_all | solution.py:14
  9.6 10.4 %all-to-all-start.1 = ((bf16[64,16,512]{2,0,1:T(8,128)(2,1)}), bf16[64,16,512]{2,0,1:T(8,128)(2,1)S(1)}, u32[]{:S(2)}, u32[]{:S(2)}) async-start(bf16[64,16,512]{2,0,1:T(8,128)(2,1)} %bitcast.29), calls=%async_computation.1 | async-start | bytes 2097152 | tf_op jit(solution)/shard_map/all_to_all | solution.py:14
  20.0 2.4 %copy.45 = bf16[8,16,8,512]{3,2,0,1:T(8,128)(2,1)} copy(bf16[8,16,8,512]{3,2,1,0:T(8,128)(2,1)} %bitcast.36) | data formatting | bytes 2097152 | tf_op jit(solution)/shard_map/all_to_all | solution.py:15
  22.4 24.3 %all-to-all-done.1 = bf16[64,16,512]{2,0,1:T(8,128)(2,1)S(1)} async-done(((bf16[64,16,512]{2,0,1:T(8,128)(2,1)}), bf16[64,16,512]{2,0,1:T(8,128)(2,1)S(1)}, u32[]{:S(2)}, u32[]{:S(2)}) %all-to-all-start.1) | async-done | bytes 1048608 | tf_op jit(solution)/shard_map/all_to_all | solution.py:14
  46.7 4.8 %all-to-all-start = ((bf16[64,16,512]{2,0,1:T(8,128)(2,1)}), bf16[64,16,512]{2,0,1:T(8,128)(2,1)S(1)}, u32[]{:S(2)}, u32[]{:S(2)}) async-start(bf16[64,16,512]{2,0,1:T(8,128)(2,1)} %bitcast.28), calls=%async_computation | async-start | bytes 2097152 | tf_op jit(solution)/shard_map/all_to_all | solution.py:15
  51.5 0.0 reduce-scatter.2.cloned.1.call-start
  51.5 0.0 copy-done.3
  51.5 0.1 copy.10
  51.6 0.1 reshape.28
  51.7 0.0 copy-done.2
  51.7 0.1 reshape.24
  51.8 0.3 reshape.23
  52.1 26.0 %all-to-all-done = bf16[64,16,512]{2,0,1:T(8,128)(2,1)S(1)} async-done(((bf16[64,16,512]{2,0,1:T(8,128)(2,1)}), bf16[64,16,512]{2,0,1:T(8,128)(2,1)S(1)}, u32[]{:S(2)}, u32[]{:S(2)}) %all-to-all-start) | async-done | bytes 1048608 | tf_op jit(solution)/shard_map/all_to_all | solution.py:15
  78.1 0.0 copy-start
  78.1 1.0 copy-done
  79.2 1.3 reshape.22
  80.5 1.4 gather_fusion.1
  82.0 1.4 gather_fusion
  83.4 0.6 fusion.11
  84.0 0.4 fusion.5
  84.4 0.5 fusion.2
  84.9 0.2 copy.17
  85.1 38.8 %all-gather.2.cloned.1.call-done = bf16[512,8192]{1,0:T(8,128)(2,1)} async-done(((bf16[512,256]{1,0:T(8,128)(2,1)}), bf16[512,8192]{1,0:T(8,128)(2,1)}) %all-gather.2.cloned.1.call-update) | async-done | bytes 8388624 | tf_op jit(solution)/shard_map/all_gather | solution.py:39
  123.9 0.0 copy-start.1
  123.9 7.7 %convolution_convert_fusion = bf16[256,8192]{1,0:T(8,128)(2,1)} fusion(bf16[512,8192]{1,0:T(8,128)(2,1)} %all-gather.2.cloned.1.call-done, bf16[32,8,4,128]{3,2,1,0:T(4,128)(2,1)S(1)} %bitcast.37), kind=kOutput, calls=%fused_computation.2 | convolution fusion | flops 2149580800 | bytes 12845056 | tf_op jit(solution)/shard_map/dot_general | solution.py:37
  131.6 0.0 reduce-scatter.2.cloned.1.call-update
  131.7 64.5 %reduce-scatter.2.cloned.1.call-done = bf16[16,8192]{1,0:T(8,128)(2,1)} async-done(((bf16[256,8192]{1,0:T(8,128)(2,1)}), bf16[16,8192]{1,0:T(8,128)(2,1)}) %reduce-scatter.2.cloned.1.call-update) | async-done | bytes 262160 | tf_op jit(solution)/shard_map/reduce_scatter | solution.py:42
  196.2 0.0 copy-done.1
  196.2 1.7 add_convert_fusion
  (2 shorter events, 0.0 us)
Async XLA Ops:
  6.5 45.0 %copy-start.3 = (s32[4,2]{0,1:T(2,128)S(1)}, s32[4,2]{0,1:T(2,128)}, u32[]{:S(2)}) copy-start(s32[4,2]{0,1:T(2,128)} %param.9) | copy-start | bytes 100
  6.5 45.2 %copy-start.2 = (bf16[256,512]{1,0:T(8,128)(2,1)S(1)}, bf16[256,512]{1,0:T(8,128)(2,1)}, u32[]{:S(2)}) copy-start(bf16[256,512]{1,0:T(8,128)(2,1)} %param.6) | copy-start | bytes 786436
  6.5 117.4 %all-gather.2.cloned.1.call-start = ((), (), s32[]{:S(2)}) async-start(), calls=%async_computation.3 | async-start | bytes 8650752 | tf_op jit(solution)/shard_map/all_gather | solution.py:39
  9.6 37.1 %all-to-all-start.1 = ((bf16[64,16,512]{2,0,1:T(8,128)(2,1)}), bf16[64,16,512]{2,0,1:T(8,128)(2,1)S(1)}, u32[]{:S(2)}, u32[]{:S(2)}) async-start(bf16[64,16,512]{2,0,1:T(8,128)(2,1)} %bitcast.29), calls=%async_computation.1 | async-start | bytes 2097152 | tf_op jit(solution)/shard_map/all_to_all | solution.py:14
  46.7 31.5 %all-to-all-start = ((bf16[64,16,512]{2,0,1:T(8,128)(2,1)}), bf16[64,16,512]{2,0,1:T(8,128)(2,1)S(1)}, u32[]{:S(2)}, u32[]{:S(2)}) async-start(bf16[64,16,512]{2,0,1:T(8,128)(2,1)} %bitcast.28), calls=%async_computation | async-start | bytes 2097152 | tf_op jit(solution)/shard_map/all_to_all | solution.py:15
  51.5 144.7 %reduce-scatter.2.cloned.1.call-start = ((), (), s32[]{:S(2)}) async-start(), calls=%async_computation.4 | async-start | bytes 4456448 | tf_op jit(solution)/shard_map/reduce_scatter | solution.py:42
  78.1 1.1 copy-start
  123.9 72.3 %copy-start.1 = (bf16[16,8192]{1,0:T(8,128)(2,1)S(1)}, bf16[16,8192]{1,0:T(8,128)(2,1)}, u32[]{:S(2)}) copy-start(bf16[16,8192]{1,0:T(8,128)(2,1)} %param.10) | copy-start | bytes 786436
Sparse Core Ops, SparseCore 0:
  10.4 113.4 all-gather.1
  131.8 64.3 reduce-scatter.1
where the time goes:
time: 205 us
  waiting for transfers between devices  154 us (75%)
  starting transfers between devices  15.3 us (7%)
  between operations  13.5 us (7%)
  local copies, waits for them, and re-layouts  10.7 us (5%)
  matrix products  8.81 us (4%)
  other arithmetic  2.14 us (1%)
    reduce_scatter x1, waiting for transfers between devices, shards(): lax.psum_scatter(partial_value.astype(jnp.bfloat16), 'tp', scatter_dimens...  64.5 us
    all_gather x1, waiting for transfers between devices, shards(): lax.all_gather(out_weight, 'rows', axis=1, tiled=True)  38.8 us
    all_to_all x1, waiting for transfers between devices, shards(): lax.all_to_all(nbr_values, 'tp', split_axis=1, concat_axis=0, tiled=True)  26 us
    all_to_all x1, waiting for transfers between devices, shards(): lax.all_to_all(nbr_keys, 'tp', split_axis=1, concat_axis=0, tiled=True)  24.3 us
    all_to_all x1, starting transfers between devices, shards(): lax.all_to_all(nbr_keys, 'tp', split_axis=1, concat_axis=0, tiled=True)  10.4 us
    dot_general x1, matrix products, shards(): jnp.dot(attn, lax.all_gather(out_weight, 'rows', axis=1, tiled=True), pre...  7.74 us
    all_to_all x1, starting transfers between devices, shards(): lax.all_to_all(nbr_values, 'tp', split_axis=1, concat_axis=0, tiled=True)  4.79 us
  transfers between devices with their start and end apart: 4, of which 4 were waited for; matrix products, arithmetic and copies ran while one was open for 5% of the time, Pallas kernels for 0%

commit v1 on v0

--- a/solution.py
+++ b/solution.py
@@ -36,7 +36,9 @@
     attn = attended.astype(jnp.bfloat16).reshape(queries.shape[0], heads_local * HD)
     partial_value = jnp.dot(
         attn,
-        lax.all_gather(out_weight, "rows", axis=1, tiled=True),
+        jnp.concatenate(
+            lax.all_to_all(jnp.stack([out_weight] * lax.axis_size("rows")), "rows", 0, 0), axis=1
+        ),
         preferred_element_type=jnp.float32,
     )
     summed = lax.psum_scatter(

time: 205 us -> 373 us (1.82)
  the two profiles are of different devices: /device:TPU:8 before, /device:TPU:2 now
where the time goes in v1:
time: 373 us
  waiting for transfers between devices  310 us (83%)
  starting transfers between devices  25.7 us (7%)
  between operations  13.5 us (4%)
  local copies, waits for them, and re-layouts  13 us (3%)
  matrix products  8.83 us (2%)
    all_to_all x1, waiting for transfers between devices, shards(): lax.all_to_all(jnp.stack([out_weight] * lax.axis_size('rows')), 'rows', 0...  183 us
    reduce_scatter x1, waiting for transfers between devices, shards(): lax.psum_scatter(partial_value.astype(jnp.bfloat16), 'tp', scatter_dimens...  75.6 us
    all_to_all x1, waiting for transfers between devices, shards(): lax.all_to_all(nbr_keys, 'tp', split_axis=1, concat_axis=0, tiled=True)  26.5 us
    all_to_all x1, waiting for transfers between devices, shards(): lax.all_to_all(nbr_values, 'tp', split_axis=1, concat_axis=0, tiled=True)  24.3 us
    all_to_all x1, starting transfers between devices, shards(): lax.all_to_all(jnp.stack([out_weight] * lax.axis_size('rows')), 'rows', 0...  10.4 us
    all_to_all x1, starting transfers between devices, shards(): lax.all_to_all(nbr_values, 'tp', split_axis=1, concat_axis=0, tiled=True)  10.4 us
    dot_general x1, matrix products, shards(): jnp.dot(attn, jnp.concatenate(lax.all_to_all(jnp.stack([out_weight] * lax...  7.76 us
  transfers between devices with their start and end apart: 4, of which 4 were waited for; matrix products, arithmetic and copies ran while one was open for 2% of the time, Pallas kernels for 0%

profile of v1, /device:TPU:2, one launch (start us, length us, event | category | flops | bytes accessed | tf_op | source)
XLA Modules:
  0.0 372.7 jit_solution(1696617779607468065)
XLA Ops:
  6.5 0.0 copy-start.1
  6.5 2.4 copy.46
  8.9 10.4 %all-to-all-start = ((bf16[64,16,512]{2,0,1:T(8,128)(2,1)}), bf16[64,16,512]{2,0,1:T(8,128)(2,1)S(1)}, u32[]{:S(2)}, u32[]{:S(2)}) async-start(bf16[64,16,512]{2,0,1:T(8,128)(2,1)} %bitcast.31), calls=%async_computation | async-start | bytes 2097152 | tf_op jit(solution)/shard_map/all_to_all | solution.py:15
  19.3 2.4 copy.47
  21.7 24.3 %all-to-all-done = bf16[64,16,512]{2,0,1:T(8,128)(2,1)S(1)} async-done(((bf16[64,16,512]{2,0,1:T(8,128)(2,1)}), bf16[64,16,512]{2,0,1:T(8,128)(2,1)S(1)}, u32[]{:S(2)}, u32[]{:S(2)}) %all-to-all-start) | async-done | bytes 1048608 | tf_op jit(solution)/shard_map/all_to_all | solution.py:15
  46.0 4.8 %all-to-all-start.1 = ((bf16[64,16,512]{2,0,1:T(8,128)(2,1)}), bf16[64,16,512]{2,0,1:T(8,128)(2,1)S(1)}, u32[]{:S(2)}, u32[]{:S(2)}) async-start(bf16[64,16,512]{2,0,1:T(8,128)(2,1)} %bitcast.32), calls=%async_computation.1 | async-start | bytes 2097152 | tf_op jit(solution)/shard_map/all_to_all | solution.py:14
  50.8 0.0 copy-done.1
  50.8 0.1 copy.18
  50.9 26.5 %all-to-all-done.1 = bf16[64,16,512]{2,0,1:T(8,128)(2,1)S(1)} async-done(((bf16[64,16,512]{2,0,1:T(8,128)(2,1)}), bf16[64,16,512]{2,0,1:T(8,128)(2,1)S(1)}, u32[]{:S(2)}, u32[]{:S(2)}) %all-to-all-start.1) | async-done | bytes 1048608 | tf_op jit(solution)/shard_map/all_to_all | solution.py:14
  77.4 4.2 %stack.2 = bf16[32,512,256]{1,2,0:T(8,128)(2,1)} broadcast(bf16[512,256]{0,1:T(8,128)(2,1)S(1)} %copy.18), dimensions={1,2} | broadcast | bytes 8650752 | tf_op jit(solution)/shard_map/stack | solution.py:40
  81.6 0.0 copy-start.3
  81.6 0.0 copy-start.2
  81.6 10.4 %all-to-all-start.2 = ((bf16[32,512,256]{1,2,0:T(8,128)(2,1)}), bf16[32,512,256]{1,2,0:T(8,128)(2,1)}, u32[]{:S(2)}, u32[]{:S(2)}) async-start(bf16[32,512,256]{1,2,0:T(8,128)(2,1)} %stack.2), calls=%async_computation.2 | async-start | bytes 16777216 | tf_op jit(solution)/shard_map/all_to_all | solution.py:40
  92.1 0.0 reduce-scatter.2.cloned.1.call-start
  92.1 0.0 copy-done.3
  92.1 0.1 copy.10
  92.2 0.1 reshape.38
  92.3 0.0 copy-done.2
  92.3 0.1 reshape.32
  92.4 0.3 reshape.30
  92.7 0.3 reshape.31
  93.0 1.4 gather_fusion
  94.4 1.4 gather_fusion.1
  95.9 0.6 fusion.11
  96.5 0.4 fusion.5
  96.9 0.5 fusion.2
  97.4 0.2 copy.17
  97.6 183.2 %all-to-all-done.2 = bf16[32,512,256]{1,2,0:T(8,128)(2,1)} async-done(((bf16[32,512,256]{1,2,0:T(8,128)(2,1)}), bf16[32,512,256]{1,2,0:T(8,128)(2,1)}, u32[]{:S(2)}, u32[]{:S(2)}) %all-to-all-start.2) | async-done | bytes 8388640 | tf_op jit(solution)/shard_map/all_to_all | solution.py:40
  280.8 0.0 copy-start
  280.8 7.8 %convolution_convert_fusion = bf16[256,8192]{1,0:T(8,128)(2,1)} fusion(bf16[512,8192]{0,1:T(8,128)(2,1)} %bitcast.10, bf16[32,8,4,128]{3,2,1,0:T(4,128)(2,1)S(1)} %bitcast.38), kind=kOutput, calls=%fused_computation.2 | convolution fusion | flops 2149580800 | bytes 12845056 | tf_op jit(solution)/shard_map/dot_general | solution.py:37
  288.5 0.0 reduce-scatter.2.cloned.1.call-update
  288.5 75.6 %reduce-scatter.2.cloned.1.call-done = bf16[16,8192]{1,0:T(8,128)(2,1)} async-done(((bf16[256,8192]{1,0:T(8,128)(2,1)}), bf16[16,8192]{1,0:T(8,128)(2,1)}) %reduce-scatter.2.cloned.1.call-update) | async-done | bytes 262160 | tf_op jit(solution)/shard_map/reduce_scatter | solution.py:44
  364.2 0.0 copy-done
  364.2 1.7 add_convert_fusion
  (2 shorter events, 0.0 us)
Async XLA Ops:
  6.5 44.2 %copy-start.1 = (bf16[512,256]{1,0:T(8,128)(2,1)S(1)}, bf16[512,256]{1,0:T(8,128)(2,1)}, u32[]{:S(2)}) copy-start(bf16[512,256]{1,0:T(8,128)(2,1)} %param.11) | copy-start | bytes 786436
  8.9 37.1 %all-to-all-start = ((bf16[64,16,512]{2,0,1:T(8,128)(2,1)}), bf16[64,16,512]{2,0,1:T(8,128)(2,1)S(1)}, u32[]{:S(2)}, u32[]{:S(2)}) async-start(bf16[64,16,512]{2,0,1:T(8,128)(2,1)} %bitcast.31), calls=%async_computation | async-start | bytes 2097152 | tf_op jit(solution)/shard_map/all_to_all | solution.py:15
  46.0 31.5 %all-to-all-start.1 = ((bf16[64,16,512]{2,0,1:T(8,128)(2,1)}), bf16[64,16,512]{2,0,1:T(8,128)(2,1)S(1)}, u32[]{:S(2)}, u32[]{:S(2)}) async-start(bf16[64,16,512]{2,0,1:T(8,128)(2,1)} %bitcast.32), calls=%async_computation.1 | async-start | bytes 2097152 | tf_op jit(solution)/shard_map/all_to_all | solution.py:14
  81.6 10.5 %copy-start.3 = (s32[4,2]{0,1:T(2,128)S(1)}, s32[4,2]{0,1:T(2,128)}, u32[]{:S(2)}) copy-start(s32[4,2]{0,1:T(2,128)} %param.9) | copy-start | bytes 100
  81.6 10.7 %copy-start.2 = (bf16[256,512]{1,0:T(8,128)(2,1)S(1)}, bf16[256,512]{1,0:T(8,128)(2,1)}, u32[]{:S(2)}) copy-start(bf16[256,512]{1,0:T(8,128)(2,1)} %param.6) | copy-start | bytes 786436
  81.6 199.1 %all-to-all-start.2 = ((bf16[32,512,256]{1,2,0:T(8,128)(2,1)}), bf16[32,512,256]{1,2,0:T(8,128)(2,1)}, u32[]{:S(2)}, u32[]{:S(2)}) async-start(bf16[32,512,256]{1,2,0:T(8,128)(2,1)} %stack.2), calls=%async_computation.2 | async-start | bytes 16777216 | tf_op jit(solution)/shard_map/all_to_all | solution.py:40
  92.1 272.1 %reduce-scatter.2.cloned.1.call-start = ((), (), s32[]{:S(2)}) async-start(), calls=%async_computation.4 | async-start | bytes 4456448 | tf_op jit(solution)/shard_map/reduce_scatter | solution.py:44
  280.8 83.4 %copy-start = (bf16[16,8192]{1,0:T(8,128)(2,1)S(1)}, bf16[16,8192]{1,0:T(8,128)(2,1)}, u32[]{:S(2)}) copy-start(bf16[16,8192]{1,0:T(8,128)(2,1)} %param.10) | copy-start | bytes 786436
Sparse Core Ops, SparseCore 0:
  288.7 75.4 reduce-scatter.1
